TPU v7x, 32 devices: a whole 2x2x4 slice. The times are simulated.
32 devices in a mesh: rows: 8 (over z, core), cols: 4 (over y, x).
Axes of the slice: x: 2, y: 2, z: 4, core: 2. Of those that a mesh axis runs over, the one named last changes fastest.
Arguments:
- markov: bfloat16 [2048, 4096], P('rows'), may hold values from -0.015625 to 0.015625
- panel: bfloat16 [131072, 256], P('rows'), may hold values from -6 to 6
Outputs:
- product: float32 [4, 4096, 256], P('cols', 'rows')
All inputs are finite; a program needn't handle non-finite values.
Results may differ from a plain program's by a relative error of at most 0.0003.
Values may be sent and summed in bfloat16 or wider, within the bound.
A program may use at most 128 MiB of HBM per device.

v0:
```python
import jax
import jax.numpy as jnp
from jax import lax
from jax.sharding import PartitionSpec as P


def from_behind(shard, axis, by):
    count = lax.axis_size(axis)
    return lax.ppermute(shard, axis, [(i, (i + by) % count) for i in range(count)])


def per_device(markov, panel):
    rows_here = markov.shape[0]
    col_count = lax.axis_size("cols")
    width_cols = rows_here // col_count
    col_index = lax.axis_index("cols")
    sensors = panel.shape[0] // rows_here
    inputs = markov.shape[1] // sensors
    panel_cols = panel.shape[1]
    base = col_index * width_cols
    span = rows_here * sensors
    after = from_behind(markov, "rows", -1)
    joined = jnp.concatenate([markov, after], 0)
    laid_out = (
        joined.reshape(2 * rows_here, sensors, inputs).transpose(2, 0, 1).reshape(inputs, 2 * span)
    )

    def one_column(index):
        tile = lax.dynamic_slice_in_dim(laid_out, index * sensors, span, 1)
        return jnp.dot(tile, panel, preferred_element_type=jnp.float32)

    owned_rows = width_cols * inputs // lax.axis_size("rows")
    needed = min(width_cols, (owned_rows * lax.axis_size("rows") + inputs - 1) // inputs + 1)
    lowest = jnp.clip(jnp.int32(0) // inputs, 0, width_cols - needed)
    indices = base + lowest + jnp.arange(needed, dtype=jnp.int32)
    blocks = lax.map(one_column, indices)
    blocks = blocks.reshape(needed * inputs, panel_cols)
    mine = lax.psum_scatter(blocks, "rows", scatter_dimension=0, tiled=True)
    return mine[None]


def solution(mesh):
    placed = (P("rows", None), P("rows", None))
    return jax.shard_map(
        per_device, mesh=mesh, in_specs=placed, out_specs=P("cols", "rows", None), check_vma=False
    )
```

profile of v0, /device:TPU:23, one launch (start us, length us, event | category | flops | bytes accessed | tf_op | source)
XLA Modules:
  0.0 595.1 jit_solution(10568208579446274208)
XLA Ops:
  10.5 25.0 %collective-permute-done = bf16[256,4096]{0,1:T(8,128)(2,1)} collective-permute-done((bf16[256,4096]{0,1:T(8,128)(2,1)S(1)}, bf16[256,4096]{0,1:T(8,128)(2,1)}, u32[]{:S(2)}, u32[]{:S(2)}) %collective-permute-start) | collective-permute-done | bytes 2097184 | tf_op jit(solution)/shard_map/ppermute | solution.py:9
  39.4 9.2 %copy.6 = bf16[64,512,64]{2,1,0:T(8,128)(2,1)} copy(bf16[64,512,64]{1,0,2:T(8,128)(2,1)} %bitcast.17) | data formatting | bytes 8388608 | tf_op jit(solution)/shard_map/transpose | solution.py:25
  48.6 10.6 %reshape.12 = bf16[64,32768]{1,0:T(8,128)(2,1)} reshape(bf16[64,512,64]{2,1,0:T(8,128)(2,1)} %copy.6) | data formatting | bytes 8388608 | tf_op jit(solution)/shard_map/reshape | solution.py:25
  59.2 478.4 %while.10 = (s32[]{:T(128)}, f32[64,64,256]{2,1,0:T(8,128)}, s32[64]{0:T(128)S(1)}, bf16[64,32768]{1,0:T(8,128)(2,1)}, bf16[16384,256]{1,0:T(8,128)(2,1)}, /*index=5*/s32[]{:T(128)}, s32[1]{0:T(128)}, s32[]{:T(128)}, s32[]{:T(128)}) while((s32[]{:T(128)}, f32[64,64,256]{2,1,0:T(8,128)}, s32[64]{0:T(128)S(1)}, bf16[64,32768]{1,0:T(8,128)(2,1)}, ...), condition=%wide.region_1.2_spmd, body=%wide.region_0.1_spmd.sunk | while | flops 536870912 | bytes 10551463 | solution.py:36
  60.5 6.2 %fusion.15 = f32[64,64,256]{2,1,0:T(8,128)} fusion(f32[64,64,256]{2,1,0:T(8,128)} %get-tuple-element.84, s32[]{:T(128)S(6)} %copy.10, bf16[16384,256]{1,0:T(8,128)(2,1)} %get-tuple-element.96, bf16[64,32768]{1,0:T(8,128)(2,1)} %get-tuple-element.95, s32[]{:T(128)S(6)} %select_n.7), kind=kOutput, calls=%fused_computation.3.clone.1 | convolution fusion | flops 536870912 | bytes 10551304 | tf_op jit(solution)/shard_map/while/body/eval_jaxpr/dot_general | solution.py:30
  68.0 6.2 %fusion.15 = f32[64,64,256]{2,1,0:T(8,128)} fusion(f32[64,64,256]{2,1,0:T(8,128)} %get-tuple-element.84, s32[]{:T(128)S(6)} %copy.10, bf16[16384,256]{1,0:T(8,128)(2,1)} %get-tuple-element.96, bf16[64,32768]{1,0:T(8,128)(2,1)} %get-tuple-element.95, s32[]{:T(128)S(6)} %select_n.7), kind=kOutput, calls=%fused_computation.3.clone.1 | convolution fusion | flops 536870912 | bytes 10551304 | tf_op jit(solution)/shard_map/while/body/eval_jaxpr/dot_general | solution.py:30
  82.9 6.2 %fusion.15 = f32[64,64,256]{2,1,0:T(8,128)} fusion(f32[64,64,256]{2,1,0:T(8,128)} %get-tuple-element.84, s32[]{:T(128)S(6)} %copy.10, bf16[16384,256]{1,0:T(8,128)(2,1)} %get-tuple-element.96, bf16[64,32768]{1,0:T(8,128)(2,1)} %get-tuple-element.95, s32[]{:T(128)S(6)} %select_n.7), kind=kOutput, calls=%fused_computation.3.clone.1 | convolution fusion | flops 536870912 | bytes 10551304 | tf_op jit(solution)/shard_map/while/body/eval_jaxpr/dot_general | solution.py:30
  90.4 6.2 %fusion.15 = f32[64,64,256]{2,1,0:T(8,128)} fusion(f32[64,64,256]{2,1,0:T(8,128)} %get-tuple-element.84, s32[]{:T(128)S(6)} %copy.10, bf16[16384,256]{1,0:T(8,128)(2,1)} %get-tuple-element.96, bf16[64,32768]{1,0:T(8,128)(2,1)} %get-tuple-element.95, s32[]{:T(128)S(6)} %select_n.7), kind=kOutput, calls=%fused_computation.3.clone.1 | convolution fusion | flops 536870912 | bytes 10551304 | tf_op jit(solution)/shard_map/while/body/eval_jaxpr/dot_general | solution.py:30
  97.9 6.2 %fusion.15 = f32[64,64,256]{2,1,0:T(8,128)} fusion(f32[64,64,256]{2,1,0:T(8,128)} %get-tuple-element.84, s32[]{:T(128)S(6)} %copy.10, bf16[16384,256]{1,0:T(8,128)(2,1)} %get-tuple-element.96, bf16[64,32768]{1,0:T(8,128)(2,1)} %get-tuple-element.95, s32[]{:T(128)S(6)} %select_n.7), kind=kOutput, calls=%fused_computation.3.clone.1 | convolution fusion | flops 536870912 | bytes 10551304 | tf_op jit(solution)/shard_map/while/body/eval_jaxpr/dot_general | solution.py:30
  105.4 6.2 %fusion.15 = f32[64,64,256]{2,1,0:T(8,128)} fusion(f32[64,64,256]{2,1,0:T(8,128)} %get-tuple-element.84, s32[]{:T(128)S(6)} %copy.10, bf16[16384,256]{1,0:T(8,128)(2,1)} %get-tuple-element.96, bf16[64,32768]{1,0:T(8,128)(2,1)} %get-tuple-element.95, s32[]{:T(128)S(6)} %select_n.7), kind=kOutput, calls=%fused_computation.3.clone.1 | convolution fusion | flops 536870912 | bytes 10551304 | tf_op jit(solution)/shard_map/while/body/eval_jaxpr/dot_general | solution.py:30
  112.8 6.2 %fusion.15 = f32[64,64,256]{2,1,0:T(8,128)} fusion(f32[64,64,256]{2,1,0:T(8,128)} %get-tuple-element.84, s32[]{:T(128)S(6)} %copy.10, bf16[16384,256]{1,0:T(8,128)(2,1)} %get-tuple-element.96, bf16[64,32768]{1,0:T(8,128)(2,1)} %get-tuple-element.95, s32[]{:T(128)S(6)} %select_n.7), kind=kOutput, calls=%fused_computation.3.clone.1 | convolution fusion | flops 536870912 | bytes 10551304 | tf_op jit(solution)/shard_map/while/body/eval_jaxpr/dot_general | solution.py:30
  120.3 6.2 %fusion.15 = f32[64,64,256]{2,1,0:T(8,128)} fusion(f32[64,64,256]{2,1,0:T(8,128)} %get-tuple-element.84, s32[]{:T(128)S(6)} %copy.10, bf16[16384,256]{1,0:T(8,128)(2,1)} %get-tuple-element.96, bf16[64,32768]{1,0:T(8,128)(2,1)} %get-tuple-element.95, s32[]{:T(128)S(6)} %select_n.7), kind=kOutput, calls=%fused_computation.3.clone.1 | convolution fusion | flops 536870912 | bytes 10551304 | tf_op jit(solution)/shard_map/while/body/eval_jaxpr/dot_general | solution.py:30
  127.8 6.2 %fusion.15 = f32[64,64,256]{2,1,0:T(8,128)} fusion(f32[64,64,256]{2,1,0:T(8,128)} %get-tuple-element.84, s32[]{:T(128)S(6)} %copy.10, bf16[16384,256]{1,0:T(8,128)(2,1)} %get-tuple-element.96, bf16[64,32768]{1,0:T(8,128)(2,1)} %get-tuple-element.95, s32[]{:T(128)S(6)} %select_n.7), kind=kOutput, calls=%fused_computation.3.clone.1 | convolution fusion | flops 536870912 | bytes 10551304 | tf_op jit(solution)/shard_map/while/body/eval_jaxpr/dot_general | solution.py:30
  135.3 6.2 %fusion.15 = f32[64,64,256]{2,1,0:T(8,128)} fusion(f32[64,64,256]{2,1,0:T(8,128)} %get-tuple-element.84, s32[]{:T(128)S(6)} %copy.10, bf16[16384,256]{1,0:T(8,128)(2,1)} %get-tuple-element.96, bf16[64,32768]{1,0:T(8,128)(2,1)} %get-tuple-element.95, s32[]{:T(128)S(6)} %select_n.7), kind=kOutput, calls=%fused_computation.3.clone.1 | convolution fusion | flops 536870912 | bytes 10551304 | tf_op jit(solution)/shard_map/while/body/eval_jaxpr/dot_general | solution.py:30
  150.2 6.2 %fusion.15 = f32[64,64,256]{2,1,0:T(8,128)} fusion(f32[64,64,256]{2,1,0:T(8,128)} %get-tuple-element.84, s32[]{:T(128)S(6)} %copy.10, bf16[16384,256]{1,0:T(8,128)(2,1)} %get-tuple-element.96, bf16[64,32768]{1,0:T(8,128)(2,1)} %get-tuple-element.95, s32[]{:T(128)S(6)} %select_n.7), kind=kOutput, calls=%fused_computation.3.clone.1 | convolution fusion | flops 536870912 | bytes 10551304 | tf_op jit(solution)/shard_map/while/body/eval_jaxpr/dot_general | solution.py:30
  157.7 6.2 %fusion.15 = f32[64,64,256]{2,1,0:T(8,128)} fusion(f32[64,64,256]{2,1,0:T(8,128)} %get-tuple-element.84, s32[]{:T(128)S(6)} %copy.10, bf16[16384,256]{1,0:T(8,128)(2,1)} %get-tuple-element.96, bf16[64,32768]{1,0:T(8,128)(2,1)} %get-tuple-element.95, s32[]{:T(128)S(6)} %select_n.7), kind=kOutput, calls=%fused_computation.3.clone.1 | convolution fusion | flops 536870912 | bytes 10551304 | tf_op jit(solution)/shard_map/while/body/eval_jaxpr/dot_general | solution.py:30
  165.2 6.2 %fusion.15 = f32[64,64,256]{2,1,0:T(8,128)} fusion(f32[64,64,256]{2,1,0:T(8,128)} %get-tuple-element.84, s32[]{:T(128)S(6)} %copy.10, bf16[16384,256]{1,0:T(8,128)(2,1)} %get-tuple-element.96, bf16[64,32768]{1,0:T(8,128)(2,1)} %get-tuple-element.95, s32[]{:T(128)S(6)} %select_n.7), kind=kOutput, calls=%fused_computation.3.clone.1 | convolution fusion | flops 536870912 | bytes 10551304 | tf_op jit(solution)/shard_map/while/body/eval_jaxpr/dot_general | solution.py:30
  172.7 6.2 %fusion.15 = f32[64,64,256]{2,1,0:T(8,128)} fusion(f32[64,64,256]{2,1,0:T(8,128)} %get-tuple-element.84, s32[]{:T(128)S(6)} %copy.10, bf16[16384,256]{1,0:T(8,128)(2,1)} %get-tuple-element.96, bf16[64,32768]{1,0:T(8,128)(2,1)} %get-tuple-element.95, s32[]{:T(128)S(6)} %select_n.7), kind=kOutput, calls=%fused_computation.3.clone.1 | convolution fusion | flops 536870912 | bytes 10551304 | tf_op jit(solution)/shard_map/while/body/eval_jaxpr/dot_general | solution.py:30
  195.1 6.2 %fusion.15 = f32[64,64,256]{2,1,0:T(8,128)} fusion(f32[64,64,256]{2,1,0:T(8,128)} %get-tuple-element.84, s32[]{:T(128)S(6)} %copy.10, bf16[16384,256]{1,0:T(8,128)(2,1)} %get-tuple-element.96, bf16[64,32768]{1,0:T(8,128)(2,1)} %get-tuple-element.95, s32[]{:T(128)S(6)} %select_n.7), kind=kOutput, calls=%fused_computation.3.clone.1 | convolution fusion | flops 536870912 | bytes 10551304 | tf_op jit(solution)/shard_map/while/body/eval_jaxpr/dot_general | solution.py:30
  202.5 6.2 %fusion.15 = f32[64,64,256]{2,1,0:T(8,128)} fusion(f32[64,64,256]{2,1,0:T(8,128)} %get-tuple-element.84, s32[]{:T(128)S(6)} %copy.10, bf16[16384,256]{1,0:T(8,128)(2,1)} %get-tuple-element.96, bf16[64,32768]{1,0:T(8,128)(2,1)} %get-tuple-element.95, s32[]{:T(128)S(6)} %select_n.7), kind=kOutput, calls=%fused_computation.3.clone.1 | convolution fusion | flops 536870912 | bytes 10551304 | tf_op jit(solution)/shard_map/while/body/eval_jaxpr/dot_general | solution.py:30
  217.5 6.2 %fusion.15 = f32[64,64,256]{2,1,0:T(8,128)} fusion(f32[64,64,256]{2,1,0:T(8,128)} %get-tuple-element.84, s32[]{:T(128)S(6)} %copy.10, bf16[16384,256]{1,0:T(8,128)(2,1)} %get-tuple-element.96, bf16[64,32768]{1,0:T(8,128)(2,1)} %get-tuple-element.95, s32[]{:T(128)S(6)} %select_n.7), kind=kOutput, calls=%fused_computation.3.clone.1 | convolution fusion | flops 536870912 | bytes 10551304 | tf_op jit(solution)/shard_map/while/body/eval_jaxpr/dot_general | solution.py:30
  225.0 6.2 %fusion.15 = f32[64,64,256]{2,1,0:T(8,128)} fusion(f32[64,64,256]{2,1,0:T(8,128)} %get-tuple-element.84, s32[]{:T(128)S(6)} %copy.10, bf16[16384,256]{1,0:T(8,128)(2,1)} %get-tuple-element.96, bf16[64,32768]{1,0:T(8,128)(2,1)} %get-tuple-element.95, s32[]{:T(128)S(6)} %select_n.7), kind=kOutput, calls=%fused_computation.3.clone.1 | convolution fusion | flops 536870912 | bytes 10551304 | tf_op jit(solution)/shard_map/while/body/eval_jaxpr/dot_general | solution.py:30
  232.4 6.2 %fusion.15 = f32[64,64,256]{2,1,0:T(8,128)} fusion(f32[64,64,256]{2,1,0:T(8,128)} %get-tuple-element.84, s32[]{:T(128)S(6)} %copy.10, bf16[16384,256]{1,0:T(8,128)(2,1)} %get-tuple-element.96, bf16[64,32768]{1,0:T(8,128)(2,1)} %get-tuple-element.95, s32[]{:T(128)S(6)} %select_n.7), kind=kOutput, calls=%fused_computation.3.clone.1 | convolution fusion | flops 536870912 | bytes 10551304 | tf_op jit(solution)/shard_map/while/body/eval_jaxpr/dot_general | solution.py:30
  239.9 6.2 %fusion.15 = f32[64,64,256]{2,1,0:T(8,128)} fusion(f32[64,64,256]{2,1,0:T(8,128)} %get-tuple-element.84, s32[]{:T(128)S(6)} %copy.10, bf16[16384,256]{1,0:T(8,128)(2,1)} %get-tuple-element.96, bf16[64,32768]{1,0:T(8,128)(2,1)} %get-tuple-element.95, s32[]{:T(128)S(6)} %select_n.7), kind=kOutput, calls=%fused_computation.3.clone.1 | convolution fusion | flops 536870912 | bytes 10551304 | tf_op jit(solution)/shard_map/while/body/eval_jaxpr/dot_general | solution.py:30
  247.4 6.2 %fusion.15 = f32[64,64,256]{2,1,0:T(8,128)} fusion(f32[64,64,256]{2,1,0:T(8,128)} %get-tuple-element.84, s32[]{:T(128)S(6)} %copy.10, bf16[16384,256]{1,0:T(8,128)(2,1)} %get-tuple-element.96, bf16[64,32768]{1,0:T(8,128)(2,1)} %get-tuple-element.95, s32[]{:T(128)S(6)} %select_n.7), kind=kOutput, calls=%fused_computation.3.clone.1 | convolution fusion | flops 536870912 | bytes 10551304 | tf_op jit(solution)/shard_map/while/body/eval_jaxpr/dot_general | solution.py:30
  262.3 6.2 %fusion.15 = f32[64,64,256]{2,1,0:T(8,128)} fusion(f32[64,64,256]{2,1,0:T(8,128)} %get-tuple-element.84, s32[]{:T(128)S(6)} %copy.10, bf16[16384,256]{1,0:T(8,128)(2,1)} %get-tuple-element.96, bf16[64,32768]{1,0:T(8,128)(2,1)} %get-tuple-element.95, s32[]{:T(128)S(6)} %select_n.7), kind=kOutput, calls=%fused_computation.3.clone.1 | convolution fusion | flops 536870912 | bytes 10551304 | tf_op jit(solution)/shard_map/while/body/eval_jaxpr/dot_general | solution.py:30
  269.8 6.2 %fusion.15 = f32[64,64,256]{2,1,0:T(8,128)} fusion(f32[64,64,256]{2,1,0:T(8,128)} %get-tuple-element.84, s32[]{:T(128)S(6)} %copy.10, bf16[16384,256]{1,0:T(8,128)(2,1)} %get-tuple-element.96, bf16[64,32768]{1,0:T(8,128)(2,1)} %get-tuple-element.95, s32[]{:T(128)S(6)} %select_n.7), kind=kOutput, calls=%fused_computation.3.clone.1 | convolution fusion | flops 536870912 | bytes 10551304 | tf_op jit(solution)/shard_map/while/body/eval_jaxpr/dot_general | solution.py:30
  277.3 6.2 %fusion.15 = f32[64,64,256]{2,1,0:T(8,128)} fusion(f32[64,64,256]{2,1,0:T(8,128)} %get-tuple-element.84, s32[]{:T(128)S(6)} %copy.10, bf16[16384,256]{1,0:T(8,128)(2,1)} %get-tuple-element.96, bf16[64,32768]{1,0:T(8,128)(2,1)} %get-tuple-element.95, s32[]{:T(128)S(6)} %select_n.7), kind=kOutput, calls=%fused_computation.3.clone.1 | convolution fusion | flops 536870912 | bytes 10551304 | tf_op jit(solution)/shard_map/while/body/eval_jaxpr/dot_general | solution.py:30
  284.8 6.2 %fusion.15 = f32[64,64,256]{2,1,0:T(8,128)} fusion(f32[64,64,256]{2,1,0:T(8,128)} %get-tuple-element.84, s32[]{:T(128)S(6)} %copy.10, bf16[16384,256]{1,0:T(8,128)(2,1)} %get-tuple-element.96, bf16[64,32768]{1,0:T(8,128)(2,1)} %get-tuple-element.95, s32[]{:T(128)S(6)} %select_n.7), kind=kOutput, calls=%fused_computation.3.clone.1 | convolution fusion | flops 536870912 | bytes 10551304 | tf_op jit(solution)/shard_map/while/body/eval_jaxpr/dot_general | solution.py:30
  307.2 6.2 %fusion.15 = f32[64,64,256]{2,1,0:T(8,128)} fusion(f32[64,64,256]{2,1,0:T(8,128)} %get-tuple-element.84, s32[]{:T(128)S(6)} %copy.10, bf16[16384,256]{1,0:T(8,128)(2,1)} %get-tuple-element.96, bf16[64,32768]{1,0:T(8,128)(2,1)} %get-tuple-element.95, s32[]{:T(128)S(6)} %select_n.7), kind=kOutput, calls=%fused_computation.3.clone.1 | convolution fusion | flops 536870912 | bytes 10551304 | tf_op jit(solution)/shard_map/while/body/eval_jaxpr/dot_general | solution.py:30
  314.7 6.2 %fusion.15 = f32[64,64,256]{2,1,0:T(8,128)} fusion(f32[64,64,256]{2,1,0:T(8,128)} %get-tuple-element.84, s32[]{:T(128)S(6)} %copy.10, bf16[16384,256]{1,0:T(8,128)(2,1)} %get-tuple-element.96, bf16[64,32768]{1,0:T(8,128)(2,1)} %get-tuple-element.95, s32[]{:T(128)S(6)} %select_n.7), kind=kOutput, calls=%fused_computation.3.clone.1 | convolution fusion | flops 536870912 | bytes 10551304 | tf_op jit(solution)/shard_map/while/body/eval_jaxpr/dot_general | solution.py:30
  322.1 6.2 %fusion.15 = f32[64,64,256]{2,1,0:T(8,128)} fusion(f32[64,64,256]{2,1,0:T(8,128)} %get-tuple-element.84, s32[]{:T(128)S(6)} %copy.10, bf16[16384,256]{1,0:T(8,128)(2,1)} %get-tuple-element.96, bf16[64,32768]{1,0:T(8,128)(2,1)} %get-tuple-element.95, s32[]{:T(128)S(6)} %select_n.7), kind=kOutput, calls=%fused_computation.3.clone.1 | convolution fusion | flops 536870912 | bytes 10551304 | tf_op jit(solution)/shard_map/while/body/eval_jaxpr/dot_general | solution.py:30
  329.6 6.2 %fusion.15 = f32[64,64,256]{2,1,0:T(8,128)} fusion(f32[64,64,256]{2,1,0:T(8,128)} %get-tuple-element.84, s32[]{:T(128)S(6)} %copy.10, bf16[16384,256]{1,0:T(8,128)(2,1)} %get-tuple-element.96, bf16[64,32768]{1,0:T(8,128)(2,1)} %get-tuple-element.95, s32[]{:T(128)S(6)} %select_n.7), kind=kOutput, calls=%fused_computation.3.clone.1 | convolution fusion | flops 536870912 | bytes 10551304 | tf_op jit(solution)/shard_map/while/body/eval_jaxpr/dot_general | solution.py:30
  337.1 6.2 %fusion.15 = f32[64,64,256]{2,1,0:T(8,128)} fusion(f32[64,64,256]{2,1,0:T(8,128)} %get-tuple-element.84, s32[]{:T(128)S(6)} %copy.10, bf16[16384,256]{1,0:T(8,128)(2,1)} %get-tuple-element.96, bf16[64,32768]{1,0:T(8,128)(2,1)} %get-tuple-element.95, s32[]{:T(128)S(6)} %select_n.7), kind=kOutput, calls=%fused_computation.3.clone.1 | convolution fusion | flops 536870912 | bytes 10551304 | tf_op jit(solution)/shard_map/while/body/eval_jaxpr/dot_general | solution.py:30
  344.6 6.2 %fusion.15 = f32[64,64,256]{2,1,0:T(8,128)} fusion(f32[64,64,256]{2,1,0:T(8,128)} %get-tuple-element.84, s32[]{:T(128)S(6)} %copy.10, bf16[16384,256]{1,0:T(8,128)(2,1)} %get-tuple-element.96, bf16[64,32768]{1,0:T(8,128)(2,1)} %get-tuple-element.95, s32[]{:T(128)S(6)} %select_n.7), kind=kOutput, calls=%fused_computation.3.clone.1 | convolution fusion | flops 536870912 | bytes 10551304 | tf_op jit(solution)/shard_map/while/body/eval_jaxpr/dot_general | solution.py:30
  359.5 6.2 %fusion.15 = f32[64,64,256]{2,1,0:T(8,128)} fusion(f32[64,64,256]{2,1,0:T(8,128)} %get-tuple-element.84, s32[]{:T(128)S(6)} %copy.10, bf16[16384,256]{1,0:T(8,128)(2,1)} %get-tuple-element.96, bf16[64,32768]{1,0:T(8,128)(2,1)} %get-tuple-element.95, s32[]{:T(128)S(6)} %select_n.7), kind=kOutput, calls=%fused_computation.3.clone.1 | convolution fusion | flops 536870912 | bytes 10551304 | tf_op jit(solution)/shard_map/while/body/eval_jaxpr/dot_general | solution.py:30
  374.5 6.2 %fusion.15 = f32[64,64,256]{2,1,0:T(8,128)} fusion(f32[64,64,256]{2,1,0:T(8,128)} %get-tuple-element.84, s32[]{:T(128)S(6)} %copy.10, bf16[16384,256]{1,0:T(8,128)(2,1)} %get-tuple-element.96, bf16[64,32768]{1,0:T(8,128)(2,1)} %get-tuple-element.95, s32[]{:T(128)S(6)} %select_n.7), kind=kOutput, calls=%fused_computation.3.clone.1 | convolution fusion | flops 536870912 | bytes 10551304 | tf_op jit(solution)/shard_map/while/body/eval_jaxpr/dot_general | solution.py:30
  389.4 6.2 %fusion.15 = f32[64,64,256]{2,1,0:T(8,128)} fusion(f32[64,64,256]{2,1,0:T(8,128)} %get-tuple-element.84, s32[]{:T(128)S(6)} %copy.10, bf16[16384,256]{1,0:T(8,128)(2,1)} %get-tuple-element.96, bf16[64,32768]{1,0:T(8,128)(2,1)} %get-tuple-element.95, s32[]{:T(128)S(6)} %select_n.7), kind=kOutput, calls=%fused_computation.3.clone.1 | convolution fusion | flops 536870912 | bytes 10551304 | tf_op jit(solution)/shard_map/while/body/eval_jaxpr/dot_general | solution.py:30
  396.9 6.2 %fusion.15 = f32[64,64,256]{2,1,0:T(8,128)} fusion(f32[64,64,256]{2,1,0:T(8,128)} %get-tuple-element.84, s32[]{:T(128)S(6)} %copy.10, bf16[16384,256]{1,0:T(8,128)(2,1)} %get-tuple-element.96, bf16[64,32768]{1,0:T(8,128)(2,1)} %get-tuple-element.95, s32[]{:T(128)S(6)} %select_n.7), kind=kOutput, calls=%fused_computation.3.clone.1 | convolution fusion | flops 536870912 | bytes 10551304 | tf_op jit(solution)/shard_map/while/body/eval_jaxpr/dot_general | solution.py:30
  404.4 6.2 %fusion.15 = f32[64,64,256]{2,1,0:T(8,128)} fusion(f32[64,64,256]{2,1,0:T(8,128)} %get-tuple-element.84, s32[]{:T(128)S(6)} %copy.10, bf16[16384,256]{1,0:T(8,128)(2,1)} %get-tuple-element.96, bf16[64,32768]{1,0:T(8,128)(2,1)} %get-tuple-element.95, s32[]{:T(128)S(6)} %select_n.7), kind=kOutput, calls=%fused_computation.3.clone.1 | convolution fusion | flops 536870912 | bytes 10551304 | tf_op jit(solution)/shard_map/while/body/eval_jaxpr/dot_general | solution.py:30
  411.9 6.2 %fusion.15 = f32[64,64,256]{2,1,0:T(8,128)} fusion(f32[64,64,256]{2,1,0:T(8,128)} %get-tuple-element.84, s32[]{:T(128)S(6)} %copy.10, bf16[16384,256]{1,0:T(8,128)(2,1)} %get-tuple-element.96, bf16[64,32768]{1,0:T(8,128)(2,1)} %get-tuple-element.95, s32[]{:T(128)S(6)} %select_n.7), kind=kOutput, calls=%fused_computation.3.clone.1 | convolution fusion | flops 536870912 | bytes 10551304 | tf_op jit(solution)/shard_map/while/body/eval_jaxpr/dot_general | solution.py:30
  441.7 6.2 %fusion.15 = f32[64,64,256]{2,1,0:T(8,128)} fusion(f32[64,64,256]{2,1,0:T(8,128)} %get-tuple-element.84, s32[]{:T(128)S(6)} %copy.10, bf16[16384,256]{1,0:T(8,128)(2,1)} %get-tuple-element.96, bf16[64,32768]{1,0:T(8,128)(2,1)} %get-tuple-element.95, s32[]{:T(128)S(6)} %select_n.7), kind=kOutput, calls=%fused_computation.3.clone.1 | convolution fusion | flops 536870912 | bytes 10551304 | tf_op jit(solution)/shard_map/while/body/eval_jaxpr/dot_general | solution.py:30
  449.2 6.2 %fusion.15 = f32[64,64,256]{2,1,0:T(8,128)} fusion(f32[64,64,256]{2,1,0:T(8,128)} %get-tuple-element.84, s32[]{:T(128)S(6)} %copy.10, bf16[16384,256]{1,0:T(8,128)(2,1)} %get-tuple-element.96, bf16[64,32768]{1,0:T(8,128)(2,1)} %get-tuple-element.95, s32[]{:T(128)S(6)} %select_n.7), kind=kOutput, calls=%fused_computation.3.clone.1 | convolution fusion | flops 536870912 | bytes 10551304 | tf_op jit(solution)/shard_map/while/body/eval_jaxpr/dot_general | solution.py:30
  456.7 6.2 %fusion.15 = f32[64,64,256]{2,1,0:T(8,128)} fusion(f32[64,64,256]{2,1,0:T(8,128)} %get-tuple-element.84, s32[]{:T(128)S(6)} %copy.10, bf16[16384,256]{1,0:T(8,128)(2,1)} %get-tuple-element.96, bf16[64,32768]{1,0:T(8,128)(2,1)} %get-tuple-element.95, s32[]{:T(128)S(6)} %select_n.7), kind=kOutput, calls=%fused_computation.3.clone.1 | convolution fusion | flops 536870912 | bytes 10551304 | tf_op jit(solution)/shard_map/while/body/eval_jaxpr/dot_general | solution.py:30
  486.6 6.2 %fusion.15 = f32[64,64,256]{2,1,0:T(8,128)} fusion(f32[64,64,256]{2,1,0:T(8,128)} %get-tuple-element.84, s32[]{:T(128)S(6)} %copy.10, bf16[16384,256]{1,0:T(8,128)(2,1)} %get-tuple-element.96, bf16[64,32768]{1,0:T(8,128)(2,1)} %get-tuple-element.95, s32[]{:T(128)S(6)} %select_n.7), kind=kOutput, calls=%fused_computation.3.clone.1 | convolution fusion | flops 536870912 | bytes 10551304 | tf_op jit(solution)/shard_map/while/body/eval_jaxpr/dot_general | solution.py:30
  516.5 6.2 %fusion.15 = f32[64,64,256]{2,1,0:T(8,128)} fusion(f32[64,64,256]{2,1,0:T(8,128)} %get-tuple-element.84, s32[]{:T(128)S(6)} %copy.10, bf16[16384,256]{1,0:T(8,128)(2,1)} %get-tuple-element.96, bf16[64,32768]{1,0:T(8,128)(2,1)} %get-tuple-element.95, s32[]{:T(128)S(6)} %select_n.7), kind=kOutput, calls=%fused_computation.3.clone.1 | convolution fusion | flops 536870912 | bytes 10551304 | tf_op jit(solution)/shard_map/while/body/eval_jaxpr/dot_general | solution.py:30
  523.9 6.2 %fusion.15 = f32[64,64,256]{2,1,0:T(8,128)} fusion(f32[64,64,256]{2,1,0:T(8,128)} %get-tuple-element.84, s32[]{:T(128)S(6)} %copy.10, bf16[16384,256]{1,0:T(8,128)(2,1)} %get-tuple-element.96, bf16[64,32768]{1,0:T(8,128)(2,1)} %get-tuple-element.95, s32[]{:T(128)S(6)} %select_n.7), kind=kOutput, calls=%fused_computation.3.clone.1 | convolution fusion | flops 536870912 | bytes 10551304 | tf_op jit(solution)/shard_map/while/body/eval_jaxpr/dot_general | solution.py:30
  537.6 50.7 %reduce-scatter.2.cloned.1.call-done = f32[512,256]{1,0:T(8,128)} async-done(((f32[4096,256]{1,0:T(8,128)}), f32[512,256]{1,0:T(8,128)}) %reduce-scatter.2.cloned.1.call-update) | async-done | bytes 524304 | tf_op jit(solution)/shard_map/reduce_scatter | solution.py:38
  (92 shorter events, 178.9 us)
Async XLA Ops:
  6.5 581.8 %reduce-scatter.2.cloned.1.call-start = ((), (), s32[]{:S(2)}) async-start(), calls=%async_computation.1 | async-start | bytes 4718592 | tf_op jit(solution)/shard_map/reduce_scatter | solution.py:38
  9.8 25.7 %collective-permute-start = (bf16[256,4096]{0,1:T(8,128)(2,1)S(1)}, bf16[256,4096]{0,1:T(8,128)(2,1)}, u32[]{:S(2)}, u32[]{:S(2)}) collective-permute-start(bf16[256,4096]{0,1:T(8,128)(2,1)S(1)} %copy.5), channel_id=1, source_target_pairs={{0,28},{4,0},{8,4},{12,8},{16,12},{20,16},{24,20},{28,24},{1,29},{... | collective-permute-start | bytes 6291464 | tf_op jit(solution)/shard_map/ppermute | solution.py:9
Sparse Core Ops, SparseCore 0:
  537.7 50.5 reduce-scatter.1
where the time goes:
time: 600 us; the launch traced here: 595 us
  matrix products  396 us (66%)
  waiting for transfers between devices  75.7 us (13%)
  local copies, waits for them, and re-layouts  64.4 us (11%)
  loops' own time  41.1 us (7%)
  between operations  13.4 us (2%)
    dot_general x64, matrix products, one_column(): return jnp.dot(tile, panel, preferred_element_type=jnp.float32)  396 us
    reduce_scatter x1, waiting for transfers between devices, per_device(): mine = lax.psum_scatter(blocks, 'rows', scatter_dimension=0, tiled=True)  50.7 us
    dynamic_slice x64, local copies, waits for them, and re-layouts, per_device(): blocks = lax.map(one_column, indices)  41.3 us
    another operation x1, loops' own time, per_device(): blocks = lax.map(one_column, indices)  41.1 us
    ppermute x1, waiting for transfers between devices, from_behind(): lax.ppermute(shard, axis, [(i, (i + by) % count) for i in range(count)])  25 us
  transfers between devices with their start and end apart: 2, of which 2 were waited for; matrix products, arithmetic and copies ran while one was open for 0% of the time, Pallas kernels for 0%

commit v1 on v0

v1 whole, which is shorter than its diff:
```python
import functools

import jax
import jax.numpy as jnp
from jax import lax
from jax.experimental import pallas as pl
from jax.experimental.pallas import tpu as pltpu
from jax.sharding import PartitionSpec as P

MESH = pl.DeviceIdType.MESH


def kernel(
    n, inputs, blocks_owned, pieces, depth,
    ll_ref, q_hbm, out_ref,
    q_ref, give, got, acc, from_left, from_right,
    q_sem, give_sem, got_sem, line_sem, left_sem, right_sem,
):
    line = n // 2
    steps = line * pieces
    chunks = q_hbm.shape[0] // depth
    per_piece = blocks_owned // pieces
    rows_piece = per_piece * inputs
    row = lax.axis_index("rows")
    here, core = row // 2, lax.rem(row, 2)
    sibling = row + 1 - 2 * core
    has_left, has_right = here > 0, here < line - 1

    def q_copy(c):
        where = pl.ds(pl.multiple_of(c * depth, depth), depth)
        return pltpu.make_async_copy(q_hbm.at[where], q_ref.at[where], q_sem.at[c])

    @pl.loop(0, chunks)
    def _(c):
        q_copy(c).start()

    barrier = pltpu.get_barrier_semaphore()

    def greet(target):
        pl.semaphore_signal(barrier, inc=1, device_id={"rows": target}, device_id_type=MESH)

    greet(sibling)
    pl.when(has_left)(lambda: greet(row - 2))
    pl.when(has_right)(lambda: greet(row + 2))
    pl.semaphore_wait(barrier, 1 + jnp.where(has_left, 1, 0) + jnp.where(has_right, 1, 0))

    def target_of(step):
        k = step // pieces
        low = here < line // 2
        h = jnp.where(low, here, line - 1 - here)
        d = jnp.where(k < line - 1 - h, line - 1 - k, jnp.where(k < line - 1, k - (line - 1 - h), h))
        return jnp.where(low, d, line - 1 - d)

    def tile(step, core_of, dst, first):
        d, piece = target_of(step), lax.rem(step, pieces)
        start = ((2 * d + core_of) * blocks_owned + piece * per_piece) * inputs
        dst[...] = jnp.zeros_like(dst)

        @pl.loop(0, chunks)
        def _(c):
            if first is not None:
                pl.when(first)(lambda: q_copy(c).wait())
            weights = q_ref[pl.ds(pl.multiple_of(c * depth, depth), depth), :]
            parts = [
                ll_ref[:, pl.ds(pl.multiple_of(start + c * depth + 2 * inputs * p, 128), depth)]
                for p in range(per_piece // 2)
            ]
            lhs = jnp.concatenate(parts, 0) if len(parts) > 1 else parts[0]
            dst[...] += jnp.dot(lhs, weights, preferred_element_type=jnp.float32)

    def give_copy(step):
        return pltpu.make_async_remote_copy(
            give.at[step], got.at[step], give_sem.at[step], got_sem.at[step],
            device_id={"rows": sibling}, device_id_type=MESH,
        )

    def right_copy(step, slot):
        return pltpu.make_async_remote_copy(
            acc.at[step], from_left.at[slot], line_sem.at[step], left_sem.at[slot],
            device_id={"rows": row + 2}, device_id_type=MESH,
        )

    def left_copy(step, slot):
        return pltpu.make_async_remote_copy(
            acc.at[step], from_right.at[slot], line_sem.at[step], right_sem.at[slot],
            device_id={"rows": row - 2}, device_id_type=MESH,
        )

    def combine(step):
        d, piece = target_of(step), lax.rem(step, pieces)
        slot = d * pieces + piece
        give_copy(step).wait_recv()
        acc[step] += got[step]

        @pl.when(jnp.logical_and(d >= here, has_left))
        def _():
            right_copy(step, slot).wait_recv()
            acc[step] += from_left[slot]

        @pl.when(jnp.logical_and(d <= here, has_right))
        def _():
            left_copy(step, slot).wait_recv()
            acc[step] += from_right[slot]

        pl.when(d > here)(lambda: right_copy(step, slot).start())
        pl.when(d < here)(lambda: left_copy(step, slot).start())

        @pl.when(d == here)
        def _():
            out_ref[pl.ds(pl.multiple_of(piece * rows_piece, rows_piece), rows_piece), :] = acc[step]

    @pl.loop(0, steps)
    def _(step):
        tile(step, 1 - core, give.at[step], step == 0)
        give_copy(step).start()
        tile(step, core, acc.at[step], None)
        pl.when(step > 0)(lambda: combine(step - 1))

    combine(steps - 1)

    @pl.loop(0, steps)
    def _(step):
        d, piece = target_of(step), lax.rem(step, pieces)
        slot = d * pieces + piece
        give_copy(step).wait_send()
        pl.when(d > here)(lambda: right_copy(step, slot).wait_send())
        pl.when(d < here)(lambda: left_copy(step, slot).wait_send())


def per_device(markov, panel):
    rows_here = markov.shape[0]
    n = lax.axis_size("rows")
    width_cols = rows_here // lax.axis_size("cols")
    sensors = panel.shape[0] // rows_here
    inputs = markov.shape[1] // sensors
    k = panel.shape[1]
    base = lax.axis_index("cols") * width_cols
    after = lax.ppermute(markov, "rows", [(i, (i - 1) % n) for i in range(n)])
    joined = jnp.concatenate([markov, after], 0)
    needed = lax.dynamic_slice_in_dim(joined, base, rows_here + width_cols, 0)
    count = rows_here + width_cols
    flat = needed.reshape(count, sensors, inputs).transpose(2, 0, 1).reshape(inputs, count * sensors)
    moved = jnp.concatenate([flat[:, sensors:], flat[:, :sensors]], 1)
    ll = jnp.concatenate([flat, moved], 0)

    blocks_owned = width_cols // n
    pieces = 2 if blocks_owned % 4 == 0 else 1
    depth = 2048
    steps = (n // 2) * pieces
    tile = (steps, blocks_owned * inputs // pieces, k)
    dma = pltpu.SemaphoreType.DMA
    mine = pl.pallas_call(
        functools.partial(kernel, n, inputs, blocks_owned, pieces, depth),
        out_shape=jax.ShapeDtypeStruct((blocks_owned * inputs, k), jnp.float32),
        in_specs=[pl.BlockSpec(memory_space=pltpu.VMEM), pl.BlockSpec(memory_space=pl.ANY)],
        out_specs=pl.BlockSpec(memory_space=pltpu.VMEM),
        scratch_shapes=[pltpu.VMEM(panel.shape, jnp.bfloat16)]
        + [pltpu.VMEM(tile, jnp.float32)] * 5
        + [dma((panel.shape[0] // depth,))]
        + [dma((steps,))] * 5,
        compiler_params=pltpu.CompilerParams(
            collective_id=0, has_side_effects=True, vmem_limit_bytes=56 * 2**20
        ),
        cost_estimate=pl.CostEstimate(
            flops=2 * width_cols * inputs * panel.shape[0] * k, bytes_accessed=16 * 2**20, transcendentals=0
        ),
    )(ll, panel)
    return mine[None]


def solution(mesh):
    placed = (P("rows", None), P("rows", None))
    return jax.shard_map(
        per_device, mesh=mesh, in_specs=placed, out_specs=P("cols", "rows", None), check_vma=False
    )
```

time: 600 us -> 127 us (0.21)
  matrix products: 396 us -> 0 us
  Pallas kernels: 0 us -> 74.4 us
  waiting for transfers between devices: 75.7 us -> 24.4 us
  local copies, waits for them, and re-layouts: 64.4 us -> 17.9 us
  loops' own time: 41.1 us -> 0 us
  between operations: 13.4 us -> 0.05 us
    dot_general x64 -> x0, matrix products: 396 us -> none  [one_column(): return jnp.dot(tile, panel, preferred_element_type=jnp.float32)]
    pallas_call x0 -> x1, Pallas kernels: none -> 74.4 us  [per_device(): pl.pallas_call(functools.partial(kernel, n, inputs, blocks_owned, pieces,...]
    reduce_scatter x1 -> x0, waiting for transfers between devices: 50.7 us -> none  [per_device(): mine = lax.psum_scatter(blocks, 'rows', scatter_dimension=0, tiled=True)]
    dynamic_slice x64 -> x0, local copies, waits for them, and re-layouts: 41.3 us -> none  [per_device(): blocks = lax.map(one_column, indices)]
    another operation x1 -> x0, loops' own time: 41.1 us -> none  [per_device(): blocks = lax.map(one_column, indices)]
  transfers between devices with their start and end apart: 2 -> 1, of which waited for: 2 -> 1; matrix products, arithmetic and copies ran while one was open for 0% -> 0% of each run, Pallas kernels for 0% -> 0%
where the time goes in v1:
time: 127 us; the launch traced here: 126 us
  Pallas kernels  74.4 us (59%)
  waiting for transfers between devices  24.4 us (19%)
  local copies, waits for them, and re-layouts  17.9 us (14%)
  other arithmetic  8.73 us (7%)
    pallas_call x1, Pallas kernels, per_device(): pl.pallas_call(functools.partial(kernel, n, inputs, blocks_owned, pieces,...  74.4 us
    ppermute x1, waiting for transfers between devices, per_device(): after = lax.ppermute(markov, 'rows', [(i, (i - 1) % n) for i in range(n)])  24.4 us
    unnamed x4, local copies, waits for them, and re-layouts  5.74 us
    reshape x1, local copies, waits for them, and re-layouts, per_device(): needed.reshape(count, sensors, inputs).transpose(2, 0, 1)  5.69 us
    transpose x1, local copies, waits for them, and re-layouts, per_device(): needed.reshape(count, sensors, inputs).transpose(2, 0, 1)  5.67 us
    concatenate x1, other arithmetic, per_device(): ll = jnp.concatenate([flat, moved], 0)  4.61 us
    concatenate x1, other arithmetic, per_device(): joined = jnp.concatenate([markov, after], 0)  4.12 us
  transfers between devices with their start and end apart: 1, of which 1 were waited for; matrix products, arithmetic and copies ran while one was open for 0% of the time, Pallas kernels for 0%

profile of v1, /device:TPU:23, one launch (start us, length us, event | category | flops | bytes accessed | tf_op | source)
XLA Modules:
  0.0 126.2 jit_solution(1881779953130666426)
XLA Ops:
  0.0 3.3 %copy.4 = bf16[256,4096]{0,1:T(8,128)(2,1)S(1)} copy(bf16[256,4096]{1,0:T(8,128)(2,1)} %param.2) | data formatting | bytes 4194304 | tf_op args[0]
  3.3 0.0 copy-start
  3.3 0.7 collective-permute-start
  4.0 0.6 copy-done
  4.6 24.4 %collective-permute-done = bf16[256,4096]{0,1:T(8,128)(2,1)} collective-permute-done((bf16[256,4096]{0,1:T(8,128)(2,1)S(1)}, bf16[256,4096]{0,1:T(8,128)(2,1)}, u32[]{:S(2)}, u32[]{:S(2)}) %collective-permute-start) | collective-permute-done | bytes 2097184 | tf_op jit(solution)/shard_map/ppermute | solution.py:138
  29.0 4.1 %fusion.1 = bf16[320,4096]{0,1:T(8,128)(2,1)S(1)} fusion(s32[]{:T(128)S(6)} %select_n.3, bf16[256,4096]{0,1:T(8,128)(2,1)} %copy-done, bf16[256,4096]{0,1:T(8,128)(2,1)} %collective-permute-done), kind=kLoop, calls=%fused_computation.4 | loop fusion | flops 5242880 | bytes 6815748 | tf_op jit(solution)/shard_map/concatenate | solution.py:139
  33.1 5.7 %copy.5 = bf16[64,320,64]{2,1,0:T(8,128)(2,1)} copy(bf16[64,320,64]{1,0,2:T(8,128)(2,1)S(1)} %bitcast.4) | data formatting | bytes 5242880 | tf_op jit(solution)/shard_map/transpose | solution.py:142
  38.8 5.7 %reshape.7 = bf16[64,20480]{1,0:T(8,128)(2,1)S(1)} reshape(bf16[64,320,64]{2,1,0:T(8,128)(2,1)} %copy.5) | data formatting | bytes 5242880 | tf_op jit(solution)/shard_map/reshape | solution.py:142
  44.5 0.7 slice.8
  45.3 4.6 %fusion.ll_ref = bf16[128,20480]{1,0:T(8,128)(2,1)} fusion(bf16[64,64]{1,0:T(8,128)(2,1)S(1)} %slice.9, bf16[64,20416]{1,0:T(8,128)(2,1)S(1)} %slice.8, bf16[64,20480]{1,0:T(8,128)(2,1)S(1)} %reshape.7), kind=kLoop, calls=%fused_computation.1 | loop fusion | flops 15728640 | bytes 10485760 | tf_op jit(solution)/shard_map/concatenate | solution.py:144
  49.9 74.4 %shard_map.28 = f32[512,256]{1,0:T(8,128)} custom-call(bf16[128,20480]{1,0:T(8,128)(2,1)} %fusion.ll_ref, bf16[16384,256]{1,0:T(8,128)(2,1)} %q_hbm.1), custom_call_target="tpu_custom_call" | custom-call | flops 34359738368 | bytes 16777216 | tf_op jit(solution)/shard_map/pallas_call | solution.py:152
  124.3 1.9 %copy.7 = f32[1,512,256]{2,1,0:T(8,128)} copy(f32[1,512,256]{2,1,0:T(8,128)} %bitcast.5) | data formatting | bytes 1048576
  (1 shorter events, 0.0 us)
Async XLA Ops:
  3.3 1.3 %copy-start = (bf16[256,4096]{0,1:T(8,128)(2,1)}, bf16[256,4096]{0,1:T(8,128)(2,1)S(1)}, u32[]{:S(2)}) copy-start(bf16[256,4096]{0,1:T(8,128)(2,1)S(1)} %copy.4) | copy-start | bytes 6291460
  3.3 25.7 %collective-permute-start = (bf16[256,4096]{0,1:T(8,128)(2,1)S(1)}, bf16[256,4096]{0,1:T(8,128)(2,1)}, u32[]{:S(2)}, u32[]{:S(2)}) collective-permute-start(bf16[256,4096]{0,1:T(8,128)(2,1)S(1)} %copy.4), channel_id=1, source_target_pairs={{0,28},{4,0},{8,4},{12,8},{16,12},{20,16},{24,20},{28,24},{1,29},{... | collective-permute-start | bytes 6291464 | tf_op jit(solution)/shard_map/ppermute | solution.py:138

commit v2 on v1

v2 whole, which is shorter than its diff:
```python
import functools

import jax
import jax.numpy as jnp
from jax import lax
from jax.experimental import pallas as pl
from jax.experimental.pallas import tpu as pltpu
from jax.sharding import PartitionSpec as P

MESH = pl.DeviceIdType.MESH


def kernel(
    n, cols, inputs, blocks_owned, pieces,
    markov_hbm, q_hbm, out_ref,
    raw, spread, expand, ll_ref,
    q_ref, give, got, acc, from_left, from_right,
    near_sem, away_sem, next_sem, q_sem, give_sem, got_sem, line_sem, left_sem, right_sem,
):
    line = n // 2
    steps = line * pieces
    per_piece = blocks_owned // pieces
    rows_piece = per_piece * inputs
    width = markov_hbm.shape[0] // cols
    sensors = q_hbm.shape[0] // markov_hbm.shape[0]
    first_depth = width * sensors
    row, col = lax.axis_index("rows"), lax.axis_index("cols")
    here, core = row // 2, lax.rem(row, 2)
    sibling = row + 1 - 2 * core
    before, behind = lax.rem(row + n - 1, n), lax.rem(row + 1, n)
    has_left, has_right = here > 0, here < line - 1

    def q_copy(part):
        where = pl.ds(0, first_depth) if part == 0 else pl.ds(first_depth, q_hbm.shape[0] - first_depth)
        return pltpu.make_async_copy(q_hbm.at[where], q_ref.at[where], q_sem.at[part])

    def near_copy(g):
        src = pl.ds(pl.multiple_of((col + g) * width, width), width)
        dst = pl.ds(pl.multiple_of(g * width, width), width)
        return pltpu.make_async_copy(markov_hbm.at[src], raw.at[dst], near_sem.at[g])

    def next_copy(e):
        src = pl.ds(pl.multiple_of(e * width, width), width)
        dst = pl.ds(pl.multiple_of((e + cols - col) * width, width), width)
        return pltpu.make_async_remote_copy(
            markov_hbm.at[src], raw.at[dst], away_sem.at[e], next_sem.at[e],
            device_id={"rows": before}, device_id_type=MESH,
        )

    @pl.loop(0, cols - col)
    def _(g):
        near_copy(g).start()

    q_copy(0).start()
    q_copy(1).start()
    barrier = pltpu.get_barrier_semaphore()

    def greet(target):
        pl.semaphore_signal(barrier, inc=1, device_id={"rows": target}, device_id_type=MESH)

    greet(before)
    greet(behind)
    pl.when(has_left)(lambda: greet(row - 2))
    pl.when(has_right)(lambda: greet(row + 2))
    pl.semaphore_wait(barrier, 2 + jnp.where(has_left, 1, 0) + jnp.where(has_right, 1, 0))

    @pl.loop(0, col + 1)
    def _(e):
        next_copy(e).start()

    lane = 128
    half = expand.shape[0] // 2
    x = lax.broadcasted_iota(jnp.int32, expand.shape, 0)
    y = lax.broadcasted_iota(jnp.int32, expand.shape, 1)
    expand[...] = jnp.where(y == jnp.where(x < half, 2 * x, 2 * (x - half) + 1), 1.0, 0.0).astype(jnp.bfloat16)
    ll_ref[:, 0:lane] = jnp.zeros((2 * inputs, lane), jnp.bfloat16)
    group = 16
    pairs = sensors // 2

    def lay_out(g):
        pl.when(col + g < cols)(lambda: near_copy(g).wait())
        pl.when(col + g >= cols)(lambda: next_copy(col + g - cols).wait_recv())

        @pl.loop(0, width // group)
        def _(i):
            at = pl.multiple_of(g * width + i * group, group)
            for c in range(pairs):
                spread[pl.ds(c, group, stride=pairs), :] = raw[
                    pl.ds(at, group), c * lane : (c + 1) * lane
                ].astype(jnp.float32)
            turned = spread[...].astype(jnp.bfloat16).T
            lhs = jnp.concatenate(
                [
                    jnp.concatenate([turned[:inputs, k * half : (k + 1) * half], turned[inputs:, k * half : (k + 1) * half]], 1)
                    for k in range(2)
                ],
                0,
            )
            done = jnp.dot(lhs, expand[...], preferred_element_type=jnp.float32).astype(jnp.bfloat16)
            for k in range(2):
                to = pl.multiple_of(lane + at * sensors + k * 2 * half, lane)
                ll_ref[0:inputs, pl.ds(to, 2 * half)] = done[k * inputs : (k + 1) * inputs]

        span = 512

        @pl.loop(0, width * sensors // span)
        def _(i):
            at = pl.multiple_of(g * width * sensors + i * span, lane)
            wide = ll_ref[0:inputs, pl.ds(at, span + lane)]
            ll_ref[inputs : 2 * inputs, pl.ds(at, span)] = wide[:, sensors : sensors + span]

    def target_of(step):
        k = step // pieces
        low = here < line // 2
        h = jnp.where(low, here, line - 1 - here)
        d = jnp.where(k < line - 1 - h, line - 1 - k, jnp.where(k < line - 1, k - (line - 1 - h), h))
        return jnp.where(low, d, line - 1 - d)

    def part_of(step, core_of, begin, depth):
        d, piece = target_of(step), lax.rem(step, pieces)
        start = ((2 * d + core_of) * blocks_owned + piece * per_piece) * inputs + lane + begin
        parts = [
            ll_ref[:, pl.ds(pl.multiple_of(start + 2 * inputs * p, lane), depth)]
            for p in range(per_piece // 2)
        ]
        lhs = jnp.concatenate(parts, 0) if len(parts) > 1 else parts[0]
        return jnp.dot(lhs, q_ref[begin : begin + depth, :], preferred_element_type=jnp.float32)

    def give_copy(step):
        return pltpu.make_async_remote_copy(
            give.at[step], got.at[step], give_sem.at[step], got_sem.at[step],
            device_id={"rows": sibling}, device_id_type=MESH,
        )

    def right_copy(step, slot):
        return pltpu.make_async_remote_copy(
            acc.at[step], from_left.at[slot], line_sem.at[step], left_sem.at[slot],
            device_id={"rows": row + 2}, device_id_type=MESH,
        )

    def left_copy(step, slot):
        return pltpu.make_async_remote_copy(
            acc.at[step], from_right.at[slot], line_sem.at[step], right_sem.at[slot],
            device_id={"rows": row - 2}, device_id_type=MESH,
        )

    def combine(step):
        d, piece = target_of(step), lax.rem(step, pieces)
        slot = d * pieces + piece
        give_copy(step).wait_recv()
        acc[step] += got[step]

        @pl.when(jnp.logical_and(d >= here, has_left))
        def _():
            right_copy(step, slot).wait_recv()
            acc[step] += from_left[slot]

        @pl.when(jnp.logical_and(d <= here, has_right))
        def _():
            left_copy(step, slot).wait_recv()
            acc[step] += from_right[slot]

        pl.when(d > here)(lambda: right_copy(step, slot).start())
        pl.when(d < here)(lambda: left_copy(step, slot).start())

        @pl.when(d == here)
        def _():
            out_ref[pl.ds(pl.multiple_of(piece * rows_piece, rows_piece), rows_piece), :] = acc[step]

    pl.loop(0, 2)(lay_out)
    q_copy(0).wait()

    @pl.loop(0, steps)
    def _(step):
        give[step] = part_of(step, 1 - core, 0, first_depth)
        acc[step] = part_of(step, core, 0, first_depth)

    pl.loop(2, cols + 1)(lay_out)
    q_copy(1).wait()
    rest = q_hbm.shape[0] - first_depth

    @pl.loop(0, steps)
    def _(step):
        give[step] += part_of(step, 1 - core, first_depth, rest)
        give_copy(step).start()
        acc[step] += part_of(step, core, first_depth, rest)
        pl.when(step > 0)(lambda: combine(step - 1))

    combine(steps - 1)

    @pl.loop(0, steps)
    def _(step):
        d, piece = target_of(step), lax.rem(step, pieces)
        slot = d * pieces + piece
        give_copy(step).wait_send()
        pl.when(d > here)(lambda: right_copy(step, slot).wait_send())
        pl.when(d < here)(lambda: left_copy(step, slot).wait_send())

    @pl.loop(0, col + 1)
    def _(e):
        next_copy(e).wait_send()


def per_device(markov, panel):
    rows_here = markov.shape[0]
    n = lax.axis_size("rows")
    width_cols = rows_here // lax.axis_size("cols")
    sensors = panel.shape[0] // rows_here
    inputs = markov.shape[1] // sensors
    k = panel.shape[1]
    cols = lax.axis_size("cols")
    blocks_owned = width_cols // n
    pieces = 2 if blocks_owned % 4 == 0 else 1
    steps = (n // 2) * pieces
    tile = (steps, blocks_owned * inputs // pieces, k)
    dma = pltpu.SemaphoreType.DMA
    mine = pl.pallas_call(
        functools.partial(kernel, n, cols, inputs, blocks_owned, pieces),
        out_shape=jax.ShapeDtypeStruct((blocks_owned * inputs, k), jnp.float32),
        in_specs=[pl.BlockSpec(memory_space=pl.ANY)] * 2,
        out_specs=pl.BlockSpec(memory_space=pltpu.VMEM),
        scratch_shapes=[
            pltpu.VMEM((rows_here + width_cols, sensors * inputs), jnp.bfloat16),
            pltpu.VMEM((16 * sensors // 2, 128), jnp.float32),
            pltpu.VMEM((8 * sensors, 8 * sensors), jnp.bfloat16),
            pltpu.VMEM((2 * inputs, 128 + (rows_here + width_cols) * sensors), jnp.bfloat16),
            pltpu.VMEM(panel.shape, jnp.bfloat16),
        ]
        + [pltpu.VMEM(tile, jnp.float32)] * 5
        + [dma((cols,))] * 3
        + [dma((2,))]
        + [dma((steps,))] * 5,
        compiler_params=pltpu.CompilerParams(
            collective_id=0, has_side_effects=True, vmem_limit_bytes=56 * 2**20
        ),
        cost_estimate=pl.CostEstimate(
            flops=2 * width_cols * inputs * panel.shape[0] * k, bytes_accessed=16 * 2**20, transcendentals=0
        ),
    )(markov, panel)
    return mine[None]


def solution(mesh):
    placed = (P("rows", None), P("rows", None))
    return jax.shard_map(
        per_device, mesh=mesh, in_specs=placed, out_specs=P("cols", "rows", None), check_vma=False
    )
```

time: 127 us -> 96.6 us (0.76)
  waiting for transfers between devices: 24.4 us -> 0 us
  Pallas kernels: 74.4 us -> 94.5 us
  local copies, waits for them, and re-layouts: 17.9 us -> 1.87 us
  other arithmetic: 8.73 us -> 0 us
    ppermute x1 -> x0, waiting for transfers between devices: 24.4 us -> none  [per_device(): after = lax.ppermute(markov, 'rows', [(i, (i - 1) % n) for i in range(n)])]
    pallas_call x1, Pallas kernels: 74.4 us -> 94.5 us  [per_device(): pl.pallas_call(functools.partial(kernel, n, cols, inputs, blocks_owned, p...]
    concatenate x2 -> x0, other arithmetic: 8.73 us -> none  [the longest x1 4.61 us: per_device(): ll = jnp.concatenate([flat, moved], 0)]
    reshape x1 -> x0, local copies, waits for them, and re-layouts: 5.69 us -> none  [per_device(): needed.reshape(count, sensors, inputs).transpose(2, 0, 1)]
    transpose x1 -> x0, local copies, waits for them, and re-layouts: 5.67 us -> none  [per_device(): needed.reshape(count, sensors, inputs).transpose(2, 0, 1)]
    unnamed x4 -> x1, local copies, waits for them, and re-layouts: 5.74 us -> 1.87 us
  transfers between devices with their start and end apart: 1 -> 0, of which waited for: 1 -> 0; matrix products, arithmetic and copies ran while one was open for 0% -> 0% of each run, Pallas kernels for 0% -> 0%
where the time goes in v2:
time: 96.6 us; the launch traced here: 96.4 us
  Pallas kernels  94.5 us (98%)
  local copies, waits for them, and re-layouts  1.87 us (2%)
    pallas_call x1, Pallas kernels, per_device(): pl.pallas_call(functools.partial(kernel, n, cols, inputs, blocks_owned, p...  94.5 us

profile of v2, /device:TPU:23, one launch (start us, length us, event | category | flops | bytes accessed | tf_op | source)
XLA Modules:
  0.0 96.4 jit_solution(6588064589683038131)
XLA Ops:
  0.0 94.5 %shard_map.28 = f32[512,256]{1,0:T(8,128)} custom-call(bf16[256,4096]{1,0:T(8,128)(2,1)} %markov_hbm.1, bf16[16384,256]{1,0:T(8,128)(2,1)} %q_hbm.1), custom_call_target="tpu_custom_call" | custom-call | flops 34359738368 | bytes 16777216 | tf_op jit(solution)/shard_map/pallas_call | solution.py:217
  94.6 1.9 %copy.4 = f32[1,512,256]{2,1,0:T(8,128)} copy(f32[1,512,256]{2,1,0:T(8,128)} %bitcast.1) | data formatting | bytes 1048576

commit v3 on v2

--- a/solution.py
+++ b/solution.py
@@ -74,7 +74,7 @@
     y = lax.broadcasted_iota(jnp.int32, expand.shape, 1)
     expand[...] = jnp.where(y == jnp.where(x < half, 2 * x, 2 * (x - half) + 1), 1.0, 0.0).astype(jnp.bfloat16)
     ll_ref[:, 0:lane] = jnp.zeros((2 * inputs, lane), jnp.bfloat16)
-    group = 16
+    group = 32
     pairs = sensors // 2
 
     def lay_out(g):
@@ -92,12 +92,12 @@
             lhs = jnp.concatenate(
                 [
                     jnp.concatenate([turned[:inputs, k * half : (k + 1) * half], turned[inputs:, k * half : (k + 1) * half]], 1)
-                    for k in range(2)
+                    for k in range(2 * group // 16)
                 ],
                 0,
             )
             done = jnp.dot(lhs, expand[...], preferred_element_type=jnp.float32).astype(jnp.bfloat16)
-            for k in range(2):
+            for k in range(2 * group // 16):
                 to = pl.multiple_of(lane + at * sensors + k * 2 * half, lane)
                 ll_ref[0:inputs, pl.ds(to, 2 * half)] = done[k * inputs : (k + 1) * inputs]
 
@@ -144,24 +144,37 @@
             device_id={"rows": row - 2}, device_id_type=MESH,
         )
 
-    def combine(step):
+    def awaits(d):
+        left = jnp.logical_and(d >= here, has_left)
+        right = jnp.logical_and(d <= here, has_right)
+        return left, right, jnp.logical_or(left, right)
+
+    def send(step, slot, d, now):
+        pl.when(jnp.logical_and(d > here, now))(lambda: right_copy(step, slot).start())
+        pl.when(jnp.logical_and(d < here, now))(lambda: left_copy(step, slot).start())
+
+    def join(step):
+        d = target_of(step)
+        give_copy(step).wait_recv()
+        acc[step] += got[step]
+        send(step, d * pieces + lax.rem(step, pieces), d, jnp.logical_not(awaits(d)[2]))
+
+    def forward(step):
         d, piece = target_of(step), lax.rem(step, pieces)
         slot = d * pieces + piece
-        give_copy(step).wait_recv()
-        acc[step] += got[step]
-
-        @pl.when(jnp.logical_and(d >= here, has_left))
+        left, right, some = awaits(d)
+
+        @pl.when(left)
         def _():
             right_copy(step, slot).wait_recv()
             acc[step] += from_left[slot]
 
-        @pl.when(jnp.logical_and(d <= here, has_right))
+        @pl.when(right)
         def _():
             left_copy(step, slot).wait_recv()
             acc[step] += from_right[slot]
 
-        pl.when(d > here)(lambda: right_copy(step, slot).start())
-        pl.when(d < here)(lambda: left_copy(step, slot).start())
+        send(step, slot, d, some)
 
         @pl.when(d == here)
         def _():
@@ -182,11 +195,14 @@
     @pl.loop(0, steps)
     def _(step):
         give[step] += part_of(step, 1 - core, first_depth, rest)
+        acc[step] += part_of(step, core, first_depth, rest)
         give_copy(step).start()
-        acc[step] += part_of(step, core, first_depth, rest)
-        pl.when(step > 0)(lambda: combine(step - 1))
-
-    combine(steps - 1)
+        pl.when(step > 0)(lambda: join(step - 1))
+        pl.when(step > 1)(lambda: forward(step - 2))
+
+    join(steps - 1)
+    forward(steps - 2)
+    forward(steps - 1)
 
     @pl.loop(0, steps)
     def _(step):
@@ -221,7 +237,7 @@
         out_specs=pl.BlockSpec(memory_space=pltpu.VMEM),
         scratch_shapes=[
             pltpu.VMEM((rows_here + width_cols, sensors * inputs), jnp.bfloat16),
-            pltpu.VMEM((16 * sensors // 2, 128), jnp.float32),
+            pltpu.VMEM((32 * sensors // 2, 128), jnp.float32),
             pltpu.VMEM((8 * sensors, 8 * sensors), jnp.bfloat16),
             pltpu.VMEM((2 * inputs, 128 + (rows_here + width_cols) * sensors), jnp.bfloat16),
             pltpu.VMEM(panel.shape, jnp.bfloat16),

time: 96.6 us -> 78.5 us (0.81)
  Pallas kernels: 94.5 us -> 75.6 us
    pallas_call x1, Pallas kernels: 94.5 us -> 75.6 us  [per_device(): pl.pallas_call(functools.partial(kernel, n, cols, inputs, blocks_owned, p...]
where the time goes in v3:
time: 78.5 us; the launch traced here: 77.5 us
  Pallas kernels  75.6 us (96%)
  local copies, waits for them, and re-layouts  1.87 us (2%)
    pallas_call x1, Pallas kernels, per_device(): pl.pallas_call(functools.partial(kernel, n, cols, inputs, blocks_owned, p...  75.6 us
    unnamed x1, local copies, waits for them, and re-layouts  1.87 us

profile of v3, /device:TPU:23, one launch (start us, length us, event | category | flops | bytes accessed | tf_op | source)
XLA Modules:
  0.0 77.5 jit_solution(10348079452978798083)
XLA Ops:
  0.0 75.6 %shard_map.28 = f32[512,256]{1,0:T(8,128)} custom-call(bf16[256,4096]{1,0:T(8,128)(2,1)} %markov_hbm.1, bf16[16384,256]{1,0:T(8,128)(2,1)} %q_hbm.1), custom_call_target="tpu_custom_call" | custom-call | flops 34359738368 | bytes 16777216 | tf_op jit(solution)/shard_map/pallas_call | solution.py:233
  75.6 1.9 %copy.4 = f32[1,512,256]{2,1,0:T(8,128)} copy(f32[1,512,256]{2,1,0:T(8,128)} %bitcast.1) | data formatting | bytes 1048576

commit v4 on v3

--- a/solution.py
+++ b/solution.py
@@ -180,22 +180,15 @@
         def _():
             out_ref[pl.ds(pl.multiple_of(piece * rows_piece, rows_piece), rows_piece), :] = acc[step]
 
-    pl.loop(0, 2)(lay_out)
+    pl.loop(0, cols + 1)(lay_out)
     q_copy(0).wait()
+    q_copy(1).wait()
+    whole = q_hbm.shape[0]
 
     @pl.loop(0, steps)
     def _(step):
-        give[step] = part_of(step, 1 - core, 0, first_depth)
-        acc[step] = part_of(step, core, 0, first_depth)
-
-    pl.loop(2, cols + 1)(lay_out)
-    q_copy(1).wait()
-    rest = q_hbm.shape[0] - first_depth
-
-    @pl.loop(0, steps)
-    def _(step):
-        give[step] += part_of(step, 1 - core, first_depth, rest)
-        acc[step] += part_of(step, core, first_depth, rest)
+        give[step] = part_of(step, 1 - core, 0, whole)
+        acc[step] = part_of(step, core, 0, whole)
         give_copy(step).start()
         pl.when(step > 0)(lambda: join(step - 1))
         pl.when(step > 1)(lambda: forward(step - 2))

time: 78.5 us -> 80.8 us (1.029)
  Pallas kernels: 75.6 us -> 77.9 us
    pallas_call x1, Pallas kernels: 75.6 us -> 77.9 us  [per_device(): pl.pallas_call(functools.partial(kernel, n, cols, inputs, blocks_owned, p...]
where the time goes in v4:
time: 80.8 us; the launch traced here: 79.8 us
  Pallas kernels  77.9 us (96%)
  local copies, waits for them, and re-layouts  1.87 us (2%)
    pallas_call x1, Pallas kernels, per_device(): pl.pallas_call(functools.partial(kernel, n, cols, inputs, blocks_owned, p...  77.9 us
    unnamed x1, local copies, waits for them, and re-layouts  1.87 us

profile of v4, /device:TPU:23, one launch (start us, length us, event | category | flops | bytes accessed | tf_op | source)
XLA Modules:
  0.0 79.8 jit_solution(11396589023796824215)
XLA Ops:
  0.0 77.9 %shard_map.28 = f32[512,256]{1,0:T(8,128)} custom-call(bf16[256,4096]{1,0:T(8,128)(2,1)} %markov_hbm.1, bf16[16384,256]{1,0:T(8,128)(2,1)} %q_hbm.1), custom_call_target="tpu_custom_call" | custom-call | flops 34359738368 | bytes 16777216 | tf_op jit(solution)/shard_map/pallas_call | solution.py:226
  77.9 1.9 %copy.4 = f32[1,512,256]{2,1,0:T(8,128)} copy(f32[1,512,256]{2,1,0:T(8,128)} %bitcast.1) | data formatting | bytes 1048576
